TPU v7x, 32 devices: a whole 2x2x4 slice. The times are simulated.
32 devices in a mesh: slab: 2 (over y), row: 8 (over z, x), sub: 2 (over core).
Axes of the slice: x: 2, y: 2, z: 4, core: 2. Of those that a mesh axis runs over, the one named last changes fastest.
Arguments:
- states: bfloat16 [8192, 1024], P(('slab', 'row'), 'sub'), parts along dimension 0, may hold values from -6 to 6
- rotation: bfloat16 [1024, 1024], P(None, 'sub'), may hold values from -0.1875 to 0.1875
- codes: int32 [8192, 64], P(('slab', 'row'), 'sub'), parts along dimension 0, may hold values from 0 to 255
- prior_codebook: float32 [128, 256, 16], P(('slab', 'sub')), parts along dimension 0, may hold values from -6 to 6
Outputs:
- codebook: float32 [128, 256, 16], P(('slab', 'sub')), parts along dimension 0
- cross: float32 [2048, 1024], P(('slab', 'row'), 'sub'), parts along dimension 0
There are 2 independent parts, one for each index of `slab`. A program takes and returns all parts, laid end to end along the dimension named above; an argument that names none is the same for every part. Nothing has to cross between parts.
All inputs are finite; a program needn't handle non-finite values.
Results may differ from a plain program's by a relative error of at most 0.0036.
Values may be sent and summed in bfloat16 or wider, within the bound.
A program may use at most 64 MiB of HBM per device.

v0:
```python
import math

import jax
import jax.numpy as jnp
from jax import lax
from jax.sharding import PartitionSpec as P

SUBDIM = 16
K = 256


def shards(states, rotation, codes, prior_codebook):
    row_keys = states.shape[0]
    local_subs = codes.shape[1]
    local_width = rotation.shape[1]
    rows_count = lax.axis_size("row")
    labels = jnp.arange(K, dtype=jnp.int32)
    full_states = lax.all_gather(states, "sub", axis=1, tiled=True)
    rotated = jnp.dot(full_states, rotation, preferred_element_type=jnp.float32).astype(
        jnp.bfloat16
    )
    owned = local_width // rows_count
    repeat = max(1, SUBDIM // owned)
    owned_codes = max(1, owned // SUBDIM)
    piece_width = owned // owned_codes
    spread_codes = jnp.repeat(codes, repeat, axis=1)
    moved_rows, moved_codes = (
        lax.all_to_all(rotated, "row", split_axis=1, concat_axis=0, tiled=True),
        lax.all_to_all(spread_codes, "row", split_axis=1, concat_axis=0, tiled=True),
    )
    all_keys = moved_rows.shape[0]
    block_rows = math.gcd(all_keys, 4096)
    block_count = all_keys // block_rows
    rows_blocks = moved_rows.reshape(block_count, block_rows, owned)
    codes_blocks = moved_codes.reshape(block_count, block_rows, moved_codes.shape[1])

    def add_block(carry, pair):
        total_sum, total_count = carry
        row_block, code_block = pair
        new_sums = []
        new_counts = []
        for which in range(owned_codes):
            onehot = (code_block[:, which][:, None] == labels[None, :]).astype(jnp.bfloat16)
            piece = row_block[:, which * piece_width : (which + 1) * piece_width]
            new_sums.append(
                lax.dot_general(
                    onehot, piece, (((0,), (0,)), ((), ())), preferred_element_type=jnp.float32
                )
            )
            new_counts.append(jnp.sum(onehot, axis=0, dtype=jnp.float32))
        return ((total_sum + jnp.stack(new_sums), total_count + jnp.stack(new_counts)), None)

    start_sum = jnp.zeros((owned_codes, K, piece_width), jnp.float32)
    start_count = jnp.zeros((owned_codes, K), jnp.float32)
    (owner_sum, owner_count), _ = lax.scan(
        add_block, (start_sum, start_count), (rows_blocks, codes_blocks)
    )
    every_sum, every_count = (
        lax.all_gather(owner_sum, "row", axis=0, tiled=True),
        lax.all_gather(owner_count, "row", axis=0, tiled=True),
    )
    pieces = SUBDIM // piece_width
    sums = (
        every_sum.reshape(local_subs, pieces, K, piece_width)
        .transpose(0, 2, 1, 3)
        .reshape(local_subs, K, SUBDIM)
    )
    counts = every_count.reshape(local_subs, pieces, K)[:, 0, :]
    codebook = (sums + prior_codebook) / (counts[:, :, None] + 1.0)
    small_book = codebook.astype(jnp.bfloat16)
    group_size = math.gcd(8, local_subs)
    group_count = local_subs // group_size
    book_groups = small_book.reshape(group_count, group_size, K, SUBDIM)
    code_groups = codes.T.reshape(group_count, group_size, row_keys)

    def lookup_group(pair):
        book_part, code_part = pair
        onehot = (code_part[:, :, None] == labels[None, None, :]).astype(jnp.bfloat16)
        found = lax.dot_general(
            onehot, book_part, (((2,), (1,)), ((0,), (0,))), preferred_element_type=jnp.float32
        )
        return found.astype(jnp.bfloat16)

    looked = lax.map(lookup_group, (book_groups, code_groups))
    rebuilt = (
        looked.reshape(local_subs, row_keys, SUBDIM)
        .transpose(1, 0, 2)
        .reshape(row_keys, local_width)
    )
    cross = lax.psum_scatter(
        lax.dot_general(
            full_states, rebuilt, (((0,), (0,)), ((), ())), preferred_element_type=jnp.float32
        ),
        "row",
        scatter_dimension=0,
        tiled=True,
    )
    return (codebook, cross)


def solution(mesh):
    placed = (
        P(("slab", "row"), "sub"),
        P(None, "sub"),
        P(("slab", "row"), "sub"),
        P(("slab", "sub"), None, None),
    )
    return jax.shard_map(
        shards,
        mesh=mesh,
        in_specs=placed,
        out_specs=(P(("slab", "sub"), None, None), P(("slab", "row"), "sub")),
        check_vma=False,
    )
```

profile of v0, /device:TPU:0, one launch (start us, length us, event | category | flops | bytes accessed | tf_op | source)
XLA Modules:
  0.0 191.2 jit_solution(11816477892968866349)
XLA Ops:
  7.2 0.0 copy-start
  7.2 0.0 all-gather.3.cloned.1.call-start
  7.2 0.7 all-gather.3.cloned.1.call-update
  7.9 1.5 all_to_all.24
  9.4 7.3 %all-to-all-start = ((s32[512,8,4]{0,2,1:T(4,128)}), s32[512,8,4]{0,2,1:T(4,128)S(1)}, u32[]{:S(2)}, u32[]{:S(2)}) async-start(s32[512,8,4]{0,2,1:T(4,128)} %all_to_all.24), calls=%async_computation | async-start | bytes 131072 | tf_op jit(solution)/shard_map/all_to_all | solution.py:29
  16.7 6.9 %all-to-all-done = s32[512,8,4]{0,2,1:T(4,128)S(1)} async-done(((s32[512,8,4]{0,2,1:T(4,128)}), s32[512,8,4]{0,2,1:T(4,128)S(1)}, u32[]{:S(2)}, u32[]{:S(2)}) %all-to-all-start) | async-done | bytes 65568 | tf_op jit(solution)/shard_map/all_to_all | solution.py:29
  23.6 0.0 all-gather.3.cloned.1.call-done
  23.6 0.0 copy-done
  23.7 2.8 %convolution_convert_fusion = bf16[512,512]{0,1:T(8,128)(2,1)} fusion(bf16[512,1024]{1,0:T(8,128)(2,1)} %all-gather.3.cloned.1.call-done, bf16[1024,512]{1,0:T(8,128)(2,1)S(1)} %copy-done), kind=kOutput, calls=%fused_computation.32 | convolution fusion | flops 537133056 | bytes 2621440 | tf_op jit(solution)/shard_map/dot_general | solution.py:19
  26.4 3.5 %all-to-all-start.1 = ((bf16[512,8,64]{0,2,1:T(8,128)(2,1)}), bf16[512,8,64]{0,2,1:T(8,128)(2,1)S(1)}, u32[]{:S(2)}, u32[]{:S(2)}) async-start(bf16[512,8,64]{0,2,1:T(8,128)(2,1)} %bitcast.3), calls=%async_computation.1 | async-start | bytes 1048576 | tf_op jit(solution)/shard_map/all_to_all | solution.py:28
  29.9 0.0 reduce-scatter.2.cloned.1.call-start
  30.0 1.9 convert_reduce_fusion
  31.8 1.9 convert_reduce_fusion.3
  33.7 1.9 convert_reduce_fusion.1
  35.6 1.9 convert_reduce_fusion.2
  37.5 30.9 %all-gather = f32[8,4,256]{2,1,0:T(4,128)S(1)} all-gather(f32[1,4,256]{2,1,0:T(4,128)S(1)} %maximum_bitcast_fusion), channel_id=1, replica_groups=mesh['slab'=2,'row'=8,'sub'=2] {'row'}, dimensions={0}, use_global_device_ids=true | all-gather | bytes 36864 | tf_op jit(solution)/shard_map/all_gather | solution.py:60
  68.4 0.0 all-to-all-done.1
  68.4 0.8 fusion.25
  69.2 0.0 copy-start.2
  69.2 0.8 fusion.24
  70.0 0.8 fusion.23
  70.8 0.8 fusion.22
  71.7 31.2 %all_gather.10 = f32[32,256,16]{1,2,0:T(8,128)S(1)} all-gather(f32[4,256,16]{1,2,0:T(8,128)S(1)} %pad_maximum_fusion), channel_id=1, replica_groups=mesh['slab'=2,'row'=8,'sub'=2] {'row'}, dimensions={0}, use_global_device_ids=true | all-gather | bytes 589824 | tf_op jit(solution)/shard_map/all_gather | solution.py:59
  102.9 0.0 copy-done.2
  102.9 0.9 fusion.30
  103.9 0.0 copy-start.1
  103.9 7.0 %while.3 = (s32[]{:T(128)}, bf16[4,8,512,16]{2,3,1,0:T(8,128)(2,1)S(1)}, s32[4,8,512]{2,1,0:T(8,128)}, bf16[4,8,256,16]{2,3,1,0:T(8,128)(2,1)S(1)}, s32[]{:T(128)}) while((s32[]{:T(128)}, bf16[4,8,512,16]{2,3,1,0:T(8,128)(2,1)S(1)}, s32[4,8,512]{2,1,0:T(8,128)}, bf16[4,8,256,16]{2,3,1,0:T(8,128)(2,1)S(1)}, s32[]{:T(128)}) %tuple.43), condition=%wide.region_5.6_spmd.clone, body=%wide.region_4.5_spmd.clone.sunk | while | flops 34668544 | bytes 246857 | solution.py:84
  103.9 0.8 dynamic-slice_bitcast_fusion.2
  104.7 1.0 fusion.39
  105.7 0.7 dynamic-slice_bitcast_fusion.2
  106.4 1.0 fusion.39
  107.4 0.7 dynamic-slice_bitcast_fusion.2
  108.1 1.0 fusion.39
  109.1 0.7 dynamic-slice_bitcast_fusion.2
  109.8 1.0 fusion.39
  110.8 0.0 copy-done.1
  110.8 2.1 %convolution_bitcast_fusion = f32[1024,512]{0,1:T(8,128)} fusion(bf16[512,512]{0,1:T(8,128)(2,1)S(1)} %bitcast.58, bf16[512,1024]{1,0:T(8,128)(2,1)S(1)} %copy-done.1), kind=kOutput, calls=%fused_computation.31 | convolution fusion | flops 536870912 | bytes 3670016 | tf_op jit(solution)/shard_map/dot_general | solution.py:91
  112.9 0.0 reduce-scatter.2.cloned.1.call-update
  112.9 69.7 %reduce-scatter.2.cloned.1.call-done = f32[128,512]{0,1:T(8,128)} async-done(((f32[1024,512]{0,1:T(8,128)}), f32[128,512]{0,1:T(8,128)}) %reduce-scatter.2.cloned.1.call-update) | async-done | bytes 262160 | tf_op jit(solution)/shard_map/reduce_scatter | solution.py:90
  182.6 1.8 copy.13
  (7 shorter events, 0.1 us)
Async XLA Ops:
  7.2 16.5 %copy-start = (bf16[1024,512]{1,0:T(8,128)(2,1)S(1)}, bf16[1024,512]{1,0:T(8,128)(2,1)}, u32[]{:S(2)}) copy-start(bf16[1024,512]{1,0:T(8,128)(2,1)} %param.7) | copy-start | bytes 3145732
  7.2 16.5 %all-gather.3.cloned.1.call-start = ((), (), s32[]{:S(2)}) async-start(), calls=%async_computation.3 | async-start | bytes 1572864 | tf_op jit(solution)/shard_map/all_gather | solution.py:18
  9.4 14.2 %all-to-all-start = ((s32[512,8,4]{0,2,1:T(4,128)}), s32[512,8,4]{0,2,1:T(4,128)S(1)}, u32[]{:S(2)}, u32[]{:S(2)}) async-start(s32[512,8,4]{0,2,1:T(4,128)} %all_to_all.24), calls=%async_computation | async-start | bytes 131072 | tf_op jit(solution)/shard_map/all_to_all | solution.py:29
  26.4 42.0 %all-to-all-start.1 = ((bf16[512,8,64]{0,2,1:T(8,128)(2,1)}), bf16[512,8,64]{0,2,1:T(8,128)(2,1)S(1)}, u32[]{:S(2)}, u32[]{:S(2)}) async-start(bf16[512,8,64]{0,2,1:T(8,128)(2,1)} %bitcast.3), calls=%async_computation.1 | async-start | bytes 1048576 | tf_op jit(solution)/shard_map/all_to_all | solution.py:28
  29.9 152.7 %reduce-scatter.2.cloned.1.call-start = ((), (), s32[]{:S(2)}) async-start(), calls=%async_computation.4 | async-start | bytes 2359296 | tf_op jit(solution)/shard_map/reduce_scatter | solution.py:90
  69.2 33.7 %copy-start.2 = (f32[32,256,16]{1,2,0:T(8,128)S(1)}, f32[32,256,16]{1,2,0:T(8,128)}, u32[]{:S(2)}) copy-start(f32[32,256,16]{1,2,0:T(8,128)} %param.9) | copy-start | bytes 1572868
  103.9 7.0 %copy-start.1 = (bf16[512,1024]{1,0:T(8,128)(2,1)S(1)}, bf16[512,1024]{1,0:T(8,128)(2,1)}, u32[]{:S(2)}) copy-start(bf16[512,1024]{1,0:T(8,128)(2,1)} %all-gather.3.cloned.1.call-done) | copy-start | bytes 3145732
Sparse Core Ops, SparseCore 0:
  9.6 11.7 all-gather.2
  113.0 69.5 reduce-scatter.1
where the time goes:
time: 192 us; the launch traced here: 191 us
  waiting for transfers between devices  77.3 us (40%)
  blocking collectives  62.1 us (32%)
  between operations  14.1 us (7%)
  matrix products  12 us (6%)
  starting transfers between devices  10.8 us (6%)
  other arithmetic  8.45 us (4%)
  local copies, waits for them, and re-layouts  6.39 us (3%)
    reduce_scatter x1, waiting for transfers between devices, shards(): lax.psum_scatter(lax.dot_general(full_states, rebuilt, (((0,), (0,)), (()...  69.7 us
    all_gather x1, blocking collectives, shards(): lax.all_gather(owner_sum, 'row', axis=0, tiled=True)  31.2 us
    all_gather x1, blocking collectives, shards(): lax.all_gather(owner_count, 'row', axis=0, tiled=True)  30.9 us
    reduce_sum x4, other arithmetic, add_block(): new_counts.append(jnp.sum(onehot, axis=0, dtype=jnp.float32))  7.48 us
    all_to_all x1, starting transfers between devices, shards(): lax.all_to_all(spread_codes, 'row', split_axis=1, concat_axis=0, tiled=True)  7.25 us
    all_to_all x1, waiting for transfers between devices, shards(): lax.all_to_all(spread_codes, 'row', split_axis=1, concat_axis=0, tiled=True)  6.9 us
    dot_general x4, matrix products, lookup_group(): lax.dot_general(onehot, book_part, (((2,), (1,)), ((0,), (0,))), preferre...  3.96 us
  transfers between devices with their start and end apart: 4, of which 2 were waited for; matrix products, arithmetic and copies ran while one was open for 4% of the time, Pallas kernels for 0%

commit v1 on v0

--- a/solution.py
+++ b/solution.py
@@ -1,8 +1,11 @@
+import functools
 import math
 
 import jax
 import jax.numpy as jnp
 from jax import lax
+from jax.experimental import pallas as pl
+from jax.experimental.pallas import tpu as pltpu
 from jax.sharding import PartitionSpec as P
 
 SUBDIM = 16
@@ -98,6 +101,269 @@
     return (codebook, cross)
 
 
+MESH = pl.DeviceIdType.MESH
+BF16 = jnp.bfloat16
+F32 = jnp.float32
+NT = (((1,), (1,)), ((), ()))
+
+
+def kernel(
+    rows_count,
+    states_ref,
+    rotation_ref,
+    codes_ref,
+    prior_ref,
+    book_ref,
+    cross_ref,
+    other,
+    states_t,
+    rotated_t,
+    onehot,
+    part,
+    pair_sum,
+    line_out,
+    line_sum,
+    small_book,
+    rebuilt_t,
+    cross_out,
+    cross_keep,
+    cross_pair,
+    cross_line_out,
+    cross_line,
+    send_sem,
+    recv_sem,
+):
+    outer = rows_count // 2
+    me = lax.axis_index("row")
+    sub = lax.axis_index("sub")
+    deep, side = me // 2, me % 2
+    mate = deep * 2 + 1 - side
+    half = states_ref.shape[1]
+    subs = codes_ref.shape[0]
+    owned = subs // rows_count
+    feats = owned * SUBDIM
+    block = cross_ref.shape[0]
+    hops = sorted(range(outer), key=lambda k: (k == 0, -min(k, outer - k)))
+    used = []
+
+    def copy(src, dst, where):
+        index = len(used)
+        made = pltpu.make_async_remote_copy(
+            src_ref=src,
+            dst_ref=dst,
+            send_sem=send_sem.at[index],
+            recv_sem=recv_sem.at[index],
+            device_id=where,
+            device_id_type=MESH,
+        )
+        made.start()
+        used.append(made)
+        return made
+
+    def line(k):
+        return lax.rem(deep + k, outer)
+
+    barrier = pltpu.get_barrier_semaphore()
+    pl.semaphore_signal(barrier, inc=1, device_id={"sub": 1 - sub}, device_id_type=MESH)
+    pl.semaphore_signal(barrier, inc=1, device_id={"row": mate}, device_id_type=MESH)
+    for k in range(1, outer):
+        pl.semaphore_signal(
+            barrier, inc=1, device_id={"row": line(k) * 2 + side}, device_id_type=MESH
+        )
+    pl.semaphore_wait(barrier, outer + 1)
+
+    swap = copy(states_ref, other, {"sub": 1 - sub})
+    total = jnp.dot(
+        states_ref[...],
+        rotation_ref[pl.ds(pl.multiple_of(sub * half, half), half), :],
+        preferred_element_type=F32,
+    )
+    swap.wait_recv()
+    total = total + jnp.dot(
+        other[...],
+        rotation_ref[pl.ds(pl.multiple_of((1 - sub) * half, half), half), :],
+        preferred_element_type=F32,
+    )
+    rotated_t[...] = total.astype(BF16).T
+
+    keys = states_ref.shape[0]
+    labels = lax.broadcasted_iota(jnp.int32, (K, keys), 0)
+    ones = jnp.ones((SUBDIM, keys), BF16)
+
+    def sum_block(owner):
+        for j in range(owned):
+            m = owner * owned + j
+            row = codes_ref[pl.ds(m, 1), :]
+            hot = jnp.where(row == labels, 1.0, 0.0).astype(BF16)
+            onehot[m] = hot
+            piece = rotated_t[pl.ds(pl.multiple_of(m * SUBDIM, SUBDIM), SUBDIM), :]
+            found = lax.dot_general(
+                jnp.concatenate([piece, ones], axis=0), hot, NT, preferred_element_type=F32
+            )
+            part[owner, j * SUBDIM : (j + 1) * SUBDIM, :] = found[:SUBDIM]
+            part[owner, feats + 2 * j : feats + 2 * j + 2, :] = found[SUBDIM : SUBDIM + 2]
+
+    pair = {}
+    for k in hops:
+        owner = line(k) * 2 + 1 - side
+        sum_block(owner)
+        pair[k] = copy(part.at[owner], pair_sum.at[k], {"row": mate})
+    for k in hops:
+        sum_block(line(k) * 2 + side)
+    lines = {}
+    mine = None
+    for k in hops:
+        pair[k].wait_recv()
+        both = part[line(k) * 2 + side] + pair_sum[k]
+        if k == 0:
+            mine = both
+        else:
+            line_out[k - 1] = both
+            lines[k] = copy(
+                line_out.at[k - 1], line_sum.at[k - 1], {"row": line(k) * 2 + side}
+            )
+
+    states_t[pl.ds(pl.multiple_of(sub * half, half), half), :] = states_ref[...].T
+    states_t[pl.ds(pl.multiple_of((1 - sub) * half, half), half), :] = other[...].T
+
+    for k in hops:
+        if k != 0:
+            lines[k].wait_recv()
+            mine = mine + line_sum[k - 1]
+    for j in range(owned):
+        own_rows = pl.ds(pl.multiple_of(me * feats, feats) + j * SUBDIM, SUBDIM)
+        fitted = (mine[j * SUBDIM : (j + 1) * SUBDIM] + prior_ref[own_rows, :]) / (
+            mine[feats + 2 * j : feats + 2 * j + 1] + 1.0
+        )
+        small_book[own_rows, :] = fitted.astype(BF16)
+
+    def book_rows(owner):
+        return small_book.at[pl.ds(pl.multiple_of(owner * feats, feats), feats), :]
+
+    along = {}
+    for k in hops:
+        if k != 0:
+            along[k] = copy(book_rows(me), book_rows(me), {"row": line(k) * 2 + side})
+    across = {0: copy(book_rows(me), book_rows(me), {"row": mate})}
+
+    def look_up(owner):
+        for j in range(owned):
+            m = owner * owned + j
+            rows = pl.ds(pl.multiple_of(m * SUBDIM, SUBDIM), SUBDIM)
+            book = small_book[rows, :]
+            book_ref[rows, :] = book.astype(F32)
+            rebuilt_t[rows, :] = jnp.dot(
+                book, onehot[m], preferred_element_type=F32
+            ).astype(BF16)
+
+    look_up(me)
+    order = [k for k in reversed(hops) if k != 0]
+    for k in order:
+        along[k].wait_recv()
+        source = lax.rem(deep + outer - k, outer) * 2 + side
+        across[k] = copy(book_rows(source), book_rows(source), {"row": mate})
+        look_up(source)
+    across[0].wait_recv()
+    look_up(mate)
+    for k in order:
+        across[k].wait_recv()
+        look_up(lax.rem(deep + outer - k, outer) * 2 + 1 - side)
+
+    def cross_block(owner):
+        rows = pl.ds(pl.multiple_of(owner * block, block), block)
+        return lax.dot_general(
+            states_t[rows, :], rebuilt_t[...], NT, preferred_element_type=F32
+        )
+
+    for k in hops:
+        cross_out[k] = cross_block(line(k) * 2 + 1 - side).astype(BF16)
+        pair[k] = copy(cross_out.at[k], cross_pair.at[k], {"row": mate})
+    for k in hops:
+        cross_keep[k] = cross_block(line(k) * 2 + side)
+    for k in hops:
+        pair[k].wait_recv()
+        both = cross_keep[k] + cross_pair[k].astype(F32)
+        if k == 0:
+            cross_ref[...] = both
+        else:
+            cross_line_out[k - 1] = both.astype(BF16)
+            lines[k] = copy(
+                cross_line_out.at[k - 1], cross_line.at[k - 1], {"row": line(k) * 2 + side}
+            )
+    for k in order:
+        lines[k].wait_recv()
+        cross_ref[...] += cross_line[k - 1].astype(F32)
+    for made in used:
+        made.wait_send()
+
+
+def fused(rows_count, states, rotation, codes, prior_codebook):
+    keys, half = states.shape
+    width = rotation.shape[1]
+    subs = codes.shape[1]
+    outer = rows_count // 2
+    feats = subs // rows_count * SUBDIM
+    tall = feats + 2 * (subs // rows_count)
+    block = rotation.shape[0] // rows_count
+    copies = 5 * outer + 1 + 3 * (outer - 1) + 8
+    vmem = pl.BlockSpec(memory_space=pltpu.VMEM)
+    book_t, cross = pl.pallas_call(
+        functools.partial(kernel, rows_count),
+        out_shape=(
+            jax.ShapeDtypeStruct((subs * SUBDIM, K), F32),
+            jax.ShapeDtypeStruct((block, width), F32),
+        ),
+        in_specs=[vmem] * 4,
+        out_specs=(vmem, vmem),
+        scratch_shapes=[
+            pltpu.VMEM((keys, half), BF16),
+            pltpu.VMEM((2 * half, keys), BF16),
+            pltpu.VMEM((width, keys), BF16),
+            pltpu.VMEM((subs, K, keys), BF16),
+            pltpu.VMEM((rows_count, tall, K), F32),
+            pltpu.VMEM((outer, tall, K), F32),
+            pltpu.VMEM((outer - 1, tall, K), F32),
+            pltpu.VMEM((outer - 1, tall, K), F32),
+            pltpu.VMEM((width, K), BF16),
+            pltpu.VMEM((width, keys), BF16),
+            pltpu.VMEM((outer, block, width), BF16),
+            pltpu.VMEM((outer, block, width), F32),
+            pltpu.VMEM((outer, block, width), BF16),
+            pltpu.VMEM((outer - 1, block, width), BF16),
+            pltpu.VMEM((outer - 1, block, width), BF16),
+            pltpu.SemaphoreType.DMA((copies,)),
+            pltpu.SemaphoreType.DMA((copies,)),
+        ],
+        compiler_params=pltpu.CompilerParams(
+            collective_id=0, has_side_effects=True, vmem_limit_bytes=48 * 1024 * 1024
+        ),
+    )(
+        states,
+        rotation,
+        codes.T,
+        prior_codebook.transpose(0, 2, 1).reshape(subs * SUBDIM, K),
+    )
+    return book_t.reshape(subs, SUBDIM, K).transpose(0, 2, 1), cross
+
+
+def pick(mesh):
+    rows_count = mesh.shape["row"]
+
+    def run(states, rotation, codes, prior_codebook):
+        fits = (
+            rows_count % 2 == 0
+            and rows_count <= 16
+            and codes.shape[1] % rows_count == 0
+            and (codes.shape[1] // rows_count * 2) % 8 == 0
+            and rotation.shape[0] % (16 * rows_count) == 0
+        )
+        if not fits:
+            return shards(states, rotation, codes, prior_codebook)
+        return fused(rows_count, states, rotation, codes, prior_codebook)
+
+    return run
+
+
 def solution(mesh):
     placed = (
         P(("slab", "row"), "sub"),
@@ -106,7 +372,7 @@
         P(("slab", "sub"), None, None),
     )
     return jax.shard_map(
-        shards,
+        pick(mesh),
         mesh=mesh,
         in_specs=placed,
         out_specs=(P(("slab", "sub"), None, None), P(("slab", "row"), "sub")),

time: 192 us -> 51.3 us (0.27)
  waiting for transfers between devices: 77.3 us -> 0 us
  blocking collectives: 62.1 us -> 0 us
  Pallas kernels: 0 us -> 44.8 us
  between operations: 14.1 us -> 0.65 us
  matrix products: 12 us -> 0 us
  starting transfers between devices: 10.8 us -> 0 us
  other arithmetic: 8.45 us -> 0 us
    reduce_scatter x1 -> x0, waiting for transfers between devices: 69.7 us -> none  [shards(): lax.psum_scatter(lax.dot_general(full_states, rebuilt, (((0,), (0,)), (()...]
    all_gather x2 -> x0, blocking collectives: 62.1 us -> none  [the longest x1 31.2 us: shards(): lax.all_gather(owner_sum, 'row', axis=0, tiled=True)]
    pallas_call x0 -> x1, Pallas kernels: none -> 44.8 us  [fused(): pl.pallas_call(functools.partial(kernel, rows_count), out_shape=(jax.Shap...]
    dot_general x10 -> x0, matrix products: 12 us -> none  [the longest x4 3.96 us: lookup_group(): lax.dot_general(onehot, book_part, (((2,), (1,)), ((0,), (0,))), preferre...]
    all_to_all x2 -> x0, starting transfers between devices: 10.7 us -> none  [the longest x1 7.25 us: shards(): lax.all_to_all(spread_codes, 'row', split_axis=1, concat_axis=0, tiled=True)]
    reduce_sum x4 -> x0, other arithmetic: 7.48 us -> none  [add_block(): new_counts.append(jnp.sum(onehot, axis=0, dtype=jnp.float32))]
    all_to_all x2 -> x0, waiting for transfers between devices: 6.91 us -> none  [the longest x1 6.9 us: shards(): lax.all_to_all(spread_codes, 'row', split_axis=1, concat_axis=0, tiled=True)]
    unnamed x7 -> x10, local copies, waits for them, and re-layouts: 1.8 us -> 5.64 us
  transfers between devices with their start and end apart: 4 -> 0, of which waited for: 2 -> 0; matrix products, arithmetic and copies ran while one was open for 4% -> 0% of each run, Pallas kernels for 0% -> 0%
where the time goes in v1:
time: 51.3 us; the launch traced here: 51 us
  Pallas kernels  44.8 us (87%)
  local copies, waits for them, and re-layouts  5.64 us (11%)
  between operations  0.65 us (1%)
    pallas_call x1, Pallas kernels, fused(): pl.pallas_call(functools.partial(kernel, rows_count), out_shape=(jax.Shap...  44.8 us
    unnamed x10, local copies, waits for them, and re-layouts  5.64 us

profile of v1, /device:TPU:0, one launch (start us, length us, event | category | flops | bytes accessed | tf_op | source)
XLA Modules:
  0.0 51.0 jit_solution(12882844377065928325)
XLA Ops:
  0.6 0.0 copy-start
  0.6 1.2 %copy-done = bf16[1024,512]{1,0:T(8,128)(2,1)S(1)} copy-done((bf16[1024,512]{1,0:T(8,128)(2,1)S(1)}, bf16[1024,512]{1,0:T(8,128)(2,1)}, u32[]{:S(2)}) %copy-start) | copy-done | bytes 1048600
  1.9 0.0 copy-start.1
  1.9 1.0 %copy-done.1 = bf16[512,512]{1,0:T(8,128)(2,1)S(1)} copy-done((bf16[512,512]{1,0:T(8,128)(2,1)S(1)}, bf16[512,512]{1,0:T(8,128)(2,1)}, u32[]{:S(2)}) %copy-start.1) | copy-done | bytes 524312
  2.9 0.0 copy-start.2
  2.9 1.0 %copy-done.2 = f32[32,256,16]{1,2,0:T(8,128)S(1)} copy-done((f32[32,256,16]{1,2,0:T(8,128)S(1)}, f32[32,256,16]{1,2,0:T(8,128)}, u32[]{:S(2)}) %copy-start.2) | copy-done | bytes 524312
  3.9 0.0 copy-start.3
  3.9 0.8 %copy-done.3 = s32[512,32]{0,1:T(8,128)S(1)} copy-done((s32[512,32]{0,1:T(8,128)S(1)}, s32[512,32]{0,1:T(8,128)}, u32[]{:S(2)}) %copy-start.3) | copy-done | bytes 65560
  4.8 44.8 %shard_map.59 = (f32[512,256]{1,0:T(8,128)S(1)}, f32[128,512]{1,0:T(8,128)S(1)}) custom-call(bf16[512,512]{1,0:T(8,128)(2,1)S(1)} %copy-done.1, bf16[1024,512]{1,0:T(8,128)(2,1)S(1)} %copy-done, s32[32,512]{1,0:T(8,128)S(1)} %bitcast.9, f32[512,256]{1,0:T(8,128)S(1)} %bitcast.8), custom_call_target="tpu_custom_call" | custom-call | tf_op jit(solution)/shard_map/pallas_call | solution.py:310
  49.5 0.8 %copy.8 = f32[32,256,16]{1,2,0:T(8,128)} copy(f32[32,256,16]{1,2,0:T(8,128)S(1)} %bitcast.7) | data formatting | bytes 1048576
  50.3 0.7 %copy.9 = f32[128,512]{1,0:T(8,128)} copy(f32[128,512]{1,0:T(8,128)S(1)} %get-tuple-element.9) | data formatting | bytes 524288
Async XLA Ops:
  0.6 1.2 %copy-start = (bf16[1024,512]{1,0:T(8,128)(2,1)S(1)}, bf16[1024,512]{1,0:T(8,128)(2,1)}, u32[]{:S(2)}) copy-start(bf16[1024,512]{1,0:T(8,128)(2,1)} %rotation_ref.1) | copy-start | bytes 3145732
  1.9 1.0 %copy-start.1 = (bf16[512,512]{1,0:T(8,128)(2,1)S(1)}, bf16[512,512]{1,0:T(8,128)(2,1)}, u32[]{:S(2)}) copy-start(bf16[512,512]{1,0:T(8,128)(2,1)} %states_ref.1) | copy-start | bytes 1572868
  2.9 1.0 %copy-start.2 = (f32[32,256,16]{1,2,0:T(8,128)S(1)}, f32[32,256,16]{1,2,0:T(8,128)}, u32[]{:S(2)}) copy-start(f32[32,256,16]{1,2,0:T(8,128)} %param.7) | copy-start | bytes 1572868
  3.9 0.8 %copy-start.3 = (s32[512,32]{0,1:T(8,128)S(1)}, s32[512,32]{0,1:T(8,128)}, u32[]{:S(2)}) copy-start(s32[512,32]{0,1:T(8,128)} %param.6) | copy-start | bytes 196612

commit v2 on v1

--- a/solution.py
+++ b/solution.py
@@ -115,35 +115,42 @@
     prior_ref,
     book_ref,
     cross_ref,
+    states_v,
+    rotation_v,
+    codes_v,
+    prior_v,
     other,
-    states_t,
+    all_states,
+    all_codes,
+    codes_i,
     rotated_t,
-    onehot,
     part,
     pair_sum,
     line_out,
     line_sum,
     small_book,
     rebuilt_t,
-    cross_out,
-    cross_keep,
-    cross_pair,
-    cross_line_out,
-    cross_line,
+    local_sem,
     send_sem,
     recv_sem,
+    out_sem,
+    pass_sem,
+    block_sem,
 ):
     outer = rows_count // 2
     me = lax.axis_index("row")
     sub = lax.axis_index("sub")
     deep, side = me // 2, me % 2
     mate = deep * 2 + 1 - side
-    half = states_ref.shape[1]
-    subs = codes_ref.shape[0]
+    keys, half = states_v.shape
+    subs = codes_v.shape[0]
     owned = subs // rows_count
     feats = owned * SUBDIM
     block = cross_ref.shape[0]
+    per_half = rows_count // 2
+    primary = me // per_half == sub
     hops = sorted(range(outer), key=lambda k: (k == 0, -min(k, outer - k)))
+    order = [k for k in reversed(hops) if k != 0]
     used = []
 
     def copy(src, dst, where):
@@ -163,39 +170,98 @@
     def line(k):
         return lax.rem(deep + k, outer)
 
+    def back(k):
+        return lax.rem(deep + outer - k, outer)
+
+    loads = []
+    for index, (src, dst) in enumerate(
+        (
+            (states_ref, states_v),
+            (codes_ref, codes_v),
+            (rotation_ref, rotation_v),
+            (prior_ref, prior_v),
+        )
+    ):
+        loads.append(pltpu.make_async_copy(src, dst, local_sem.at[index]))
+        loads[-1].start()
+
     barrier = pltpu.get_barrier_semaphore()
     pl.semaphore_signal(barrier, inc=1, device_id={"sub": 1 - sub}, device_id_type=MESH)
-    pl.semaphore_signal(barrier, inc=1, device_id={"row": mate}, device_id_type=MESH)
-    for k in range(1, outer):
+    for k in range(1, rows_count):
         pl.semaphore_signal(
-            barrier, inc=1, device_id={"row": line(k) * 2 + side}, device_id_type=MESH
-        )
-    pl.semaphore_wait(barrier, outer + 1)
-
-    swap = copy(states_ref, other, {"sub": 1 - sub})
+            barrier, inc=1, device_id={"row": lax.rem(me + k, rows_count)}, device_id_type=MESH
+        )
+    pl.semaphore_wait(barrier, rows_count)
+
+    loads[0].wait()
+    swap = copy(states_v, other, {"sub": 1 - sub})
+
+    def columns(q):
+        return states_v.at[:, pl.ds(pl.multiple_of(q * block, block), block)]
+
+    def give(q):
+        owner = sub * per_half + q
+        return pltpu.make_async_remote_copy(
+            src_ref=columns(q),
+            dst_ref=all_states.at[me],
+            send_sem=out_sem.at[q],
+            recv_sem=block_sem.at[me],
+            device_id={"row": owner},
+            device_id_type=MESH,
+        )
+
+    def forward(source):
+        return pltpu.make_async_remote_copy(
+            src_ref=all_states.at[source],
+            dst_ref=all_states.at[source],
+            send_sem=pass_sem.at[source],
+            recv_sem=block_sem.at[source],
+            device_id={"sub": 1 - sub},
+            device_id_type=MESH,
+        )
+
+    loads[1].wait()
+    all_codes[me] = codes_v[...].astype(F32).astype(BF16)
+    codes_along = {}
+    for k in hops:
+        if k != 0:
+            codes_along[k] = copy(
+                all_codes.at[me], all_codes.at[me], {"row": line(k) * 2 + side}
+            )
+    codes_across = {0: copy(all_codes.at[me], all_codes.at[me], {"row": mate})}
+    for q in range(per_half):
+
+        @pl.when(sub * per_half + q != me)
+        def _():
+            give(q).start()
+
+    @pl.when(primary)
+    def _():
+        all_states[me] = columns(lax.rem(me, per_half))[...]
+        forward(me).start()
+
+    loads[2].wait()
     total = jnp.dot(
-        states_ref[...],
-        rotation_ref[pl.ds(pl.multiple_of(sub * half, half), half), :],
+        states_v[...],
+        rotation_v[pl.ds(pl.multiple_of(sub * half, half), half), :],
         preferred_element_type=F32,
     )
     swap.wait_recv()
     total = total + jnp.dot(
         other[...],
-        rotation_ref[pl.ds(pl.multiple_of((1 - sub) * half, half), half), :],
+        rotation_v[pl.ds(pl.multiple_of((1 - sub) * half, half), half), :],
         preferred_element_type=F32,
     )
     rotated_t[...] = total.astype(BF16).T
 
-    keys = states_ref.shape[0]
     labels = lax.broadcasted_iota(jnp.int32, (K, keys), 0)
     ones = jnp.ones((SUBDIM, keys), BF16)
 
     def sum_block(owner):
         for j in range(owned):
             m = owner * owned + j
-            row = codes_ref[pl.ds(m, 1), :]
+            row = codes_v[pl.ds(m, 1), :]
             hot = jnp.where(row == labels, 1.0, 0.0).astype(BF16)
-            onehot[m] = hot
             piece = rotated_t[pl.ds(pl.multiple_of(m * SUBDIM, SUBDIM), SUBDIM), :]
             found = lax.dot_general(
                 jnp.concatenate([piece, ones], axis=0), hot, NT, preferred_element_type=F32
@@ -222,17 +288,18 @@
             lines[k] = copy(
                 line_out.at[k - 1], line_sum.at[k - 1], {"row": line(k) * 2 + side}
             )
-
-    states_t[pl.ds(pl.multiple_of(sub * half, half), half), :] = states_ref[...].T
-    states_t[pl.ds(pl.multiple_of((1 - sub) * half, half), half), :] = other[...].T
-
+    for k in order:
+        codes_along[k].wait_recv()
+        source = back(k) * 2 + side
+        codes_across[k] = copy(all_codes.at[source], all_codes.at[source], {"row": mate})
+    loads[3].wait()
     for k in hops:
         if k != 0:
             lines[k].wait_recv()
             mine = mine + line_sum[k - 1]
     for j in range(owned):
         own_rows = pl.ds(pl.multiple_of(me * feats, feats) + j * SUBDIM, SUBDIM)
-        fitted = (mine[j * SUBDIM : (j + 1) * SUBDIM] + prior_ref[own_rows, :]) / (
+        fitted = (mine[j * SUBDIM : (j + 1) * SUBDIM] + prior_v[own_rows, :]) / (
             mine[feats + 2 * j : feats + 2 * j + 1] + 1.0
         )
         small_book[own_rows, :] = fitted.astype(BF16)
@@ -245,54 +312,76 @@
         if k != 0:
             along[k] = copy(book_rows(me), book_rows(me), {"row": line(k) * 2 + side})
     across = {0: copy(book_rows(me), book_rows(me), {"row": mate})}
+
+    for k in range(1, rows_count):
+        source = lax.rem(me + k, rows_count)
+        forward(source).wait_recv()
+
+        @pl.when(primary)
+        def _():
+            forward(source).start()
+
+    for k in order:
+        codes_across[k].wait_recv()
+    codes_across[0].wait_recv()
 
     def look_up(owner):
         for j in range(owned):
             m = owner * owned + j
             rows = pl.ds(pl.multiple_of(m * SUBDIM, SUBDIM), SUBDIM)
-            book = small_book[rows, :]
-            book_ref[rows, :] = book.astype(F32)
-            rebuilt_t[rows, :] = jnp.dot(
-                book, onehot[m], preferred_element_type=F32
-            ).astype(BF16)
-
+            book_ref[rows, :] = small_book[rows, :].astype(F32)
+
+        @pl.loop(0, rows_count)
+        def _(source):
+            base = pl.multiple_of(owner * owned, owned)
+            for j in range(owned):
+                rows = pl.ds(pl.multiple_of((base + j) * SUBDIM, SUBDIM), SUBDIM)
+                row = all_codes_f(source, base, j)
+                hot = jnp.where(row == labels, 1.0, 0.0).astype(BF16)
+                rebuilt_t[source, rows, :] = jnp.dot(
+                    small_book[rows, :], hot, preferred_element_type=F32
+                ).astype(BF16)
+
+    def all_codes_f(source, base, j):
+        return codes_i[source, pl.ds(base + j, 1), :]
+
+    for source in range(rows_count):
+        codes_i[source] = all_codes[source].astype(F32).astype(jnp.int32)
     look_up(me)
-    order = [k for k in reversed(hops) if k != 0]
     for k in order:
         along[k].wait_recv()
-        source = lax.rem(deep + outer - k, outer) * 2 + side
+        source = back(k) * 2 + side
         across[k] = copy(book_rows(source), book_rows(source), {"row": mate})
-        look_up(source)
+    for k in order:
+        look_up(back(k) * 2 + side)
     across[0].wait_recv()
     look_up(mate)
     for k in order:
         across[k].wait_recv()
-        look_up(lax.rem(deep + outer - k, outer) * 2 + 1 - side)
-
-    def cross_block(owner):
-        rows = pl.ds(pl.multiple_of(owner * block, block), block)
-        return lax.dot_general(
-            states_t[rows, :], rebuilt_t[...], NT, preferred_element_type=F32
-        )
-
-    for k in hops:
-        cross_out[k] = cross_block(line(k) * 2 + 1 - side).astype(BF16)
-        pair[k] = copy(cross_out.at[k], cross_pair.at[k], {"row": mate})
-    for k in hops:
-        cross_keep[k] = cross_block(line(k) * 2 + side)
-    for k in hops:
-        pair[k].wait_recv()
-        both = cross_keep[k] + cross_pair[k].astype(F32)
-        if k == 0:
-            cross_ref[...] = both
-        else:
-            cross_line_out[k - 1] = both.astype(BF16)
-            lines[k] = copy(
-                cross_line_out.at[k - 1], cross_line.at[k - 1], {"row": line(k) * 2 + side}
-            )
-    for k in order:
-        lines[k].wait_recv()
-        cross_ref[...] += cross_line[k - 1].astype(F32)
+        look_up(back(k) * 2 + 1 - side)
+
+    @pl.when(jnp.logical_not(primary))
+    def _():
+        forward(me).wait_recv()
+
+    total = jnp.zeros(cross_ref.shape, F32)
+    for source in range(rows_count):
+        total = total + lax.dot_general(
+            all_states[source].T, rebuilt_t[source], NT, preferred_element_type=F32
+        )
+    cross_ref[...] = total
+
+    for q in range(per_half):
+
+        @pl.when(sub * per_half + q != me)
+        def _():
+            give(q).wait_send()
+
+    @pl.when(primary)
+    def _():
+        for source in range(rows_count):
+            forward(source).wait_send()
+
     for made in used:
         made.wait_send()
 
@@ -305,7 +394,7 @@
     feats = subs // rows_count * SUBDIM
     tall = feats + 2 * (subs // rows_count)
     block = rotation.shape[0] // rows_count
-    copies = 5 * outer + 1 + 3 * (outer - 1) + 8
+    copies = 7 * outer
     vmem = pl.BlockSpec(memory_space=pltpu.VMEM)
     book_t, cross = pl.pallas_call(
         functools.partial(kernel, rows_count),
@@ -313,26 +402,30 @@
             jax.ShapeDtypeStruct((subs * SUBDIM, K), F32),
             jax.ShapeDtypeStruct((block, width), F32),
         ),
-        in_specs=[vmem] * 4,
+        in_specs=[pl.BlockSpec(memory_space=pl.ANY)] * 4,
         out_specs=(vmem, vmem),
         scratch_shapes=[
             pltpu.VMEM((keys, half), BF16),
-            pltpu.VMEM((2 * half, keys), BF16),
+            pltpu.VMEM((2 * half, width), BF16),
+            pltpu.VMEM((subs, keys), jnp.int32),
+            pltpu.VMEM((width, K), F32),
+            pltpu.VMEM((keys, half), BF16),
+            pltpu.VMEM((rows_count, keys, block), BF16),
+            pltpu.VMEM((rows_count, subs, keys), BF16),
+            pltpu.VMEM((rows_count, subs, keys), jnp.int32),
             pltpu.VMEM((width, keys), BF16),
-            pltpu.VMEM((subs, K, keys), BF16),
             pltpu.VMEM((rows_count, tall, K), F32),
             pltpu.VMEM((outer, tall, K), F32),
             pltpu.VMEM((outer - 1, tall, K), F32),
             pltpu.VMEM((outer - 1, tall, K), F32),
             pltpu.VMEM((width, K), BF16),
-            pltpu.VMEM((width, keys), BF16),
-            pltpu.VMEM((outer, block, width), BF16),
-            pltpu.VMEM((outer, block, width), F32),
-            pltpu.VMEM((outer, block, width), BF16),
-            pltpu.VMEM((outer - 1, block, width), BF16),
-            pltpu.VMEM((outer - 1, block, width), BF16),
+            pltpu.VMEM((rows_count, width, keys), BF16),
+            pltpu.SemaphoreType.DMA((4,)),
             pltpu.SemaphoreType.DMA((copies,)),
             pltpu.SemaphoreType.DMA((copies,)),
+            pltpu.SemaphoreType.DMA((outer,)),
+            pltpu.SemaphoreType.DMA((rows_count,)),
+            pltpu.SemaphoreType.DMA((rows_count,)),
         ],
         compiler_params=pltpu.CompilerParams(
             collective_id=0, has_side_effects=True, vmem_limit_bytes=48 * 1024 * 1024

time: 51.3 us -> 54.5 us (1.062)
  Pallas kernels: 44.8 us -> 47.8 us
    pallas_call x1, Pallas kernels: 44.8 us -> 47.8 us  [fused(): pl.pallas_call(functools.partial(kernel, rows_count), out_shape=(jax.Shap...]
where the time goes in v2:
time: 54.5 us; the launch traced here: 54.1 us
  Pallas kernels  47.8 us (88%)
  local copies, waits for them, and re-layouts  5.64 us (10%)
  between operations  0.65 us (1%)
    pallas_call x1, Pallas kernels, fused(): pl.pallas_call(functools.partial(kernel, rows_count), out_shape=(jax.Shap...  47.8 us
    unnamed x10, local copies, waits for them, and re-layouts  5.64 us

profile of v2, /device:TPU:0, one launch (start us, length us, event | category | flops | bytes accessed | tf_op | source)
XLA Modules:
  0.0 54.1 jit_solution(14504770665430487115)
XLA Ops:
  0.6 0.0 copy-start
  0.6 1.2 %copy-done = bf16[1024,512]{1,0:T(8,128)(2,1)S(1)} copy-done((bf16[1024,512]{1,0:T(8,128)(2,1)S(1)}, bf16[1024,512]{1,0:T(8,128)(2,1)}, u32[]{:S(2)}) %copy-start) | copy-done | bytes 1048600
  1.9 0.0 copy-start.1
  1.9 1.0 %copy-done.1 = bf16[512,512]{1,0:T(8,128)(2,1)S(1)} copy-done((bf16[512,512]{1,0:T(8,128)(2,1)S(1)}, bf16[512,512]{1,0:T(8,128)(2,1)}, u32[]{:S(2)}) %copy-start.1) | copy-done | bytes 524312
  2.9 0.0 copy-start.2
  2.9 1.0 %copy-done.2 = f32[32,256,16]{1,2,0:T(8,128)S(1)} copy-done((f32[32,256,16]{1,2,0:T(8,128)S(1)}, f32[32,256,16]{1,2,0:T(8,128)}, u32[]{:S(2)}) %copy-start.2) | copy-done | bytes 524312
  3.9 0.0 copy-start.3
  3.9 0.8 %copy-done.3 = s32[512,32]{0,1:T(8,128)S(1)} copy-done((s32[512,32]{0,1:T(8,128)S(1)}, s32[512,32]{0,1:T(8,128)}, u32[]{:S(2)}) %copy-start.3) | copy-done | bytes 65560
  4.8 47.8 %shard_map.59 = (f32[512,256]{1,0:T(8,128)S(1)}, f32[128,512]{1,0:T(8,128)S(1)}) custom-call(bf16[512,512]{1,0:T(8,128)(2,1)S(1)} %copy-done.1, bf16[1024,512]{1,0:T(8,128)(2,1)S(1)} %copy-done, s32[32,512]{1,0:T(8,128)S(1)} %bitcast.9, f32[512,256]{1,0:T(8,128)S(1)} %bitcast.8), custom_call_target="tpu_custom_call" | custom-call | tf_op jit(solution)/shard_map/pallas_call | solution.py:399
  52.6 0.8 %copy.8 = f32[32,256,16]{1,2,0:T(8,128)} copy(f32[32,256,16]{1,2,0:T(8,128)S(1)} %bitcast.7) | data formatting | bytes 1048576
  53.4 0.7 %copy.9 = f32[128,512]{1,0:T(8,128)} copy(f32[128,512]{1,0:T(8,128)S(1)} %get-tuple-element.9) | data formatting | bytes 524288
Async XLA Ops:
  0.6 1.2 %copy-start = (bf16[1024,512]{1,0:T(8,128)(2,1)S(1)}, bf16[1024,512]{1,0:T(8,128)(2,1)}, u32[]{:S(2)}) copy-start(bf16[1024,512]{1,0:T(8,128)(2,1)} %rotation_ref.1) | copy-start | bytes 3145732
  1.9 1.0 %copy-start.1 = (bf16[512,512]{1,0:T(8,128)(2,1)S(1)}, bf16[512,512]{1,0:T(8,128)(2,1)}, u32[]{:S(2)}) copy-start(bf16[512,512]{1,0:T(8,128)(2,1)} %states_ref.1) | copy-start | bytes 1572868
  2.9 1.0 %copy-start.2 = (f32[32,256,16]{1,2,0:T(8,128)S(1)}, f32[32,256,16]{1,2,0:T(8,128)}, u32[]{:S(2)}) copy-start(f32[32,256,16]{1,2,0:T(8,128)} %param.7) | copy-start | bytes 1572868
  3.9 0.8 %copy-start.3 = (s32[512,32]{0,1:T(8,128)S(1)}, s32[512,32]{0,1:T(8,128)}, u32[]{:S(2)}) copy-start(s32[512,32]{0,1:T(8,128)} %param.6) | copy-start | bytes 196612

commit v3 on v2

--- a/solution.py
+++ b/solution.py
@@ -105,6 +105,13 @@
 BF16 = jnp.bfloat16
 F32 = jnp.float32
 NT = (((1,), (1,)), ((), ()))
+
+
+LANES = 128
+
+
+def pick_lanes(table, at):
+    return jnp.take_along_axis(table, at, axis=1, mode="promise_in_bounds")
 
 
 def kernel(
@@ -229,7 +236,8 @@
                 all_codes.at[me], all_codes.at[me], {"row": line(k) * 2 + side}
             )
     codes_across = {0: copy(all_codes.at[me], all_codes.at[me], {"row": mate})}
-    for q in range(per_half):
+    for turn in range(per_half):
+        q = lax.rem(me + turn, per_half)
 
         @pl.when(sub * per_half + q != me)
         def _():
@@ -326,24 +334,30 @@
     codes_across[0].wait_recv()
 
     def look_up(owner):
-        for j in range(owned):
-            m = owner * owned + j
-            rows = pl.ds(pl.multiple_of(m * SUBDIM, SUBDIM), SUBDIM)
+        base = pl.multiple_of(owner * owned, owned)
+        spans = [
+            pl.ds(pl.multiple_of((base + j) * SUBDIM, SUBDIM), SUBDIM) for j in range(owned)
+        ]
+        for rows in spans:
             book_ref[rows, :] = small_book[rows, :].astype(F32)
 
-        @pl.loop(0, rows_count)
+        @pl.loop(0, rows_count, unroll=8)
         def _(source):
-            base = pl.multiple_of(owner * owned, owned)
-            for j in range(owned):
-                rows = pl.ds(pl.multiple_of((base + j) * SUBDIM, SUBDIM), SUBDIM)
-                row = all_codes_f(source, base, j)
-                hot = jnp.where(row == labels, 1.0, 0.0).astype(BF16)
-                rebuilt_t[source, rows, :] = jnp.dot(
-                    small_book[rows, :], hot, preferred_element_type=F32
-                ).astype(BF16)
-
-    def all_codes_f(source, base, j):
-        return codes_i[source, pl.ds(base + j, 1), :]
+            for j, rows in enumerate(spans):
+                row = codes_i[source, pl.ds(base + j, 1), :]
+                for c in range(keys // LANES):
+                    code = jnp.broadcast_to(row[:, c * LANES : (c + 1) * LANES], (8, LANES))
+                    upper = code >= LANES
+                    at = jnp.where(upper, code - LANES, code)
+                    found = []
+                    for h in range(SUBDIM // 8):
+                        part_rows = pl.ds(pl.multiple_of((base + j) * SUBDIM, SUBDIM) + 8 * h, 8)
+                        low = book_ref[part_rows, :LANES]
+                        high = book_ref[part_rows, LANES:]
+                        found.append(jnp.where(upper, pick_lanes(high, at), pick_lanes(low, at)))
+                    rebuilt_t[source, rows, c * LANES : (c + 1) * LANES] = jnp.concatenate(
+                        found, axis=0
+                    ).astype(BF16)
 
     for source in range(rows_count):
         codes_i[source] = all_codes[source].astype(F32).astype(jnp.int32)

time: 54.5 us -> 44.7 us (0.82)
  Pallas kernels: 47.8 us -> 38.1 us
    pallas_call x1, Pallas kernels: 47.8 us -> 38.1 us  [fused(): pl.pallas_call(functools.partial(kernel, rows_count), out_shape=(jax.Shap...]
where the time goes in v3:
time: 44.7 us; the launch traced here: 44.4 us
  Pallas kernels  38.1 us (85%)
  local copies, waits for them, and re-layouts  5.64 us (13%)
  between operations  0.65 us (1%)
    pallas_call x1, Pallas kernels, fused(): pl.pallas_call(functools.partial(kernel, rows_count), out_shape=(jax.Shap...  38.1 us
    unnamed x10, local copies, waits for them, and re-layouts  5.64 us

profile of v3, /device:TPU:0, one launch (start us, length us, event | category | flops | bytes accessed | tf_op | source)
XLA Modules:
  0.0 44.4 jit_solution(2630197271446840597)
XLA Ops:
  0.6 0.0 copy-start
  0.6 1.2 %copy-done = bf16[1024,512]{1,0:T(8,128)(2,1)S(1)} copy-done((bf16[1024,512]{1,0:T(8,128)(2,1)S(1)}, bf16[1024,512]{1,0:T(8,128)(2,1)}, u32[]{:S(2)}) %copy-start) | copy-done | bytes 1048600
  1.9 0.0 copy-start.1
  1.9 1.0 %copy-done.1 = bf16[512,512]{1,0:T(8,128)(2,1)S(1)} copy-done((bf16[512,512]{1,0:T(8,128)(2,1)S(1)}, bf16[512,512]{1,0:T(8,128)(2,1)}, u32[]{:S(2)}) %copy-start.1) | copy-done | bytes 524312
  2.9 0.0 copy-start.2
  2.9 1.0 %copy-done.2 = f32[32,256,16]{1,2,0:T(8,128)S(1)} copy-done((f32[32,256,16]{1,2,0:T(8,128)S(1)}, f32[32,256,16]{1,2,0:T(8,128)}, u32[]{:S(2)}) %copy-start.2) | copy-done | bytes 524312
  3.9 0.0 copy-start.3
  3.9 0.8 %copy-done.3 = s32[512,32]{0,1:T(8,128)S(1)} copy-done((s32[512,32]{0,1:T(8,128)S(1)}, s32[512,32]{0,1:T(8,128)}, u32[]{:S(2)}) %copy-start.3) | copy-done | bytes 65560
  4.8 38.1 %shard_map.59 = (f32[512,256]{1,0:T(8,128)S(1)}, f32[128,512]{1,0:T(8,128)S(1)}) custom-call(bf16[512,512]{1,0:T(8,128)(2,1)S(1)} %copy-done.1, bf16[1024,512]{1,0:T(8,128)(2,1)S(1)} %copy-done, s32[32,512]{1,0:T(8,128)S(1)} %bitcast.9, f32[512,256]{1,0:T(8,128)S(1)} %bitcast.8), custom_call_target="tpu_custom_call" | custom-call | tf_op jit(solution)/shard_map/pallas_call | solution.py:413
  42.9 0.8 %copy.8 = f32[32,256,16]{1,2,0:T(8,128)} copy(f32[32,256,16]{1,2,0:T(8,128)S(1)} %bitcast.7) | data formatting | bytes 1048576
  43.7 0.7 %copy.9 = f32[128,512]{1,0:T(8,128)} copy(f32[128,512]{1,0:T(8,128)S(1)} %get-tuple-element.9) | data formatting | bytes 524288
Async XLA Ops:
  0.6 1.2 %copy-start = (bf16[1024,512]{1,0:T(8,128)(2,1)S(1)}, bf16[1024,512]{1,0:T(8,128)(2,1)}, u32[]{:S(2)}) copy-start(bf16[1024,512]{1,0:T(8,128)(2,1)} %rotation_ref.1) | copy-start | bytes 3145732
  1.9 1.0 %copy-start.1 = (bf16[512,512]{1,0:T(8,128)(2,1)S(1)}, bf16[512,512]{1,0:T(8,128)(2,1)}, u32[]{:S(2)}) copy-start(bf16[512,512]{1,0:T(8,128)(2,1)} %states_ref.1) | copy-start | bytes 1572868
  2.9 1.0 %copy-start.2 = (f32[32,256,16]{1,2,0:T(8,128)S(1)}, f32[32,256,16]{1,2,0:T(8,128)}, u32[]{:S(2)}) copy-start(f32[32,256,16]{1,2,0:T(8,128)} %param.7) | copy-start | bytes 1572868
  3.9 0.8 %copy-start.3 = (s32[512,32]{0,1:T(8,128)S(1)}, s32[512,32]{0,1:T(8,128)}, u32[]{:S(2)}) copy-start(s32[512,32]{0,1:T(8,128)} %param.6) | copy-start | bytes 196612
